TPU v7x, 32 devices: a whole 2x2x4 slice. The times are simulated.
32 devices in a mesh: seq: 4 (over y, x), res: 8 (over z, core).
Axes of the slice: x: 2, y: 2, z: 4, core: 2. Of those that a mesh axis runs over, the one named last changes fastest.
Arguments:
- alignment_tensor: float32 [192, 128, 256], P('seq', 'res'), may hold values from -24 to 24
- standardizer_factors: float32 [3, 256], replicated, may hold values from 0.25 to 1.75
- standardizer_offsets: float32 [3, 256], replicated, may hold values from -3 to 3
- horizontal_entry_matrix: bfloat16 [256, 1024], replicated, may hold values from -4 to 4
- horizontal_sigmoid_offset: float32 [256], replicated, may hold values from -4 to 4
- horizontal_exit_matrix: bfloat16 [256, 256], replicated, may hold values from -1 to 1
- horizontal_exit_offset: float32 [256], replicated, may hold values from -2 to 2
- vertical_entry_matrix: bfloat16 [256, 1024], replicated, may hold values from -4 to 4
- vertical_sigmoid_offset: float32 [256], replicated, may hold values from -4 to 4
- vertical_exit_matrix: bfloat16 [256, 256], replicated, may hold values from -1 to 1
- vertical_exit_offset: float32 [256], replicated, may hold values from -2 to 2
- feedforward_first_matrix: bfloat16 [256, 1024], replicated, may hold values from -0.375 to 0.375
- feedforward_first_offset: float32 [1024], replicated, may hold values from -3 to 3
- feedforward_second_matrix: bfloat16 [1024, 256], replicated, may hold values from -0.25 to 0.25
- feedforward_second_offset: float32 [256], replicated, may hold values from -2 to 2
Outputs:
- updated_msa: float32 [192, 128, 256], P('seq', 'res')
All inputs are finite; a program needn't handle non-finite values.
Results may differ from a plain program's by a relative error of at most 0.012.
Values may be sent and summed in bfloat16 or wider, within the bound.
A program may use at most 64 MiB of HBM per device.

v0:
```python
import functools

import jax
import jax.numpy as jnp
from jax import lax
from jax.experimental import pallas as pl
from jax.experimental.pallas import tpu as pltpu
from jax.sharding import PartitionSpec as P

HEADS = 8
EPS = 1e-05
F32 = jnp.float32
BF16 = jnp.bfloat16
MESH = pl.DeviceIdType.MESH


def standardize(values, gain, shift):
    mean = jnp.mean(values, axis=-1, keepdims=True)
    centred = values - mean
    variance = jnp.mean(centred * centred, axis=-1, keepdims=True)
    return (centred * lax.rsqrt(variance + EPS) * gain + shift).astype(BF16)


def dot(left, right):
    return jnp.dot(left, right, preferred_element_type=F32)


def dot_nt(left, right):
    return lax.dot_general(left, right, (((1,), (1,)), ((), ())), preferred_element_type=F32)


def attend(normed, entry, value_turned, gate_offset, exit_matrix, mixed):
    length, channels = normed.shape
    size = channels // HEADS
    query = (dot(normed, entry[:, :channels]) * size ** (-0.5)).astype(BF16)
    key = dot(normed, entry[:, channels : 2 * channels]).astype(BF16)
    value = dot_nt(value_turned, normed).astype(BF16)
    gate = jax.nn.sigmoid(dot(normed, entry[:, 3 * channels :]) + gate_offset)
    lane = lax.broadcasted_iota(jnp.int32, (1, channels), 1)

    def one_head(head, own_values):
        low = head * size
        mask = jnp.where((lane >= low) & (lane < low + size), 1.0, 0.0).astype(BF16)
        scores = dot_nt(key * mask, query)
        weights = jnp.exp(scores - jnp.max(scores, axis=0, keepdims=True))
        total = jnp.sum(weights, axis=0, keepdims=True)
        return dot(own_values, weights.astype(BF16)) / total

    if length <= 256:
        outs = [one_head(h, value[h * size : (h + 1) * size]) for h in range(HEADS)]
        turned = jnp.concatenate(outs, axis=0)
    else:
        held, out = mixed
        held[...] = value

        def step(head, carry):
            rows = pl.ds(pl.multiple_of(head * size, size), size)
            out[rows, :] = one_head(head, held[rows, :])
            return carry

        lax.fori_loop(0, HEADS, step, 0)
        turned = out[...]
    gated = (gate * turned.T).astype(BF16)
    return dot(gated, exit_matrix)


def block(
    res_count,
    seq_count,
    x_ref,
    gains,
    shifts,
    row_gate,
    row_shift,
    col_gate,
    col_shift,
    ff_first_shift,
    ff_second_shift,
    row_entry_hbm,
    row_exit_hbm,
    col_entry_hbm,
    col_exit_hbm,
    ff_first_hbm,
    ff_second_hbm,
    out_ref,
    row_entry,
    row_exit,
    col_entry,
    col_exit,
    ff_first,
    ff_second,
    turned_value,
    row_sent,
    row_in,
    row_out,
    row_back,
    after_row,
    after_turned,
    col_sent,
    col_in,
    col_out,
    col_back,
    mixed_row,
    mixed_col,
    load_sem,
    sems,
    col_sems,
):
    me_res = lax.axis_index("res")
    me_seq = lax.axis_index("seq")
    groups, group = x_ref.shape[1], x_ref.shape[2]
    res_local, channels = x_ref.shape[3], x_ref.shape[4]
    seq_local = after_row.shape[0]
    items = groups * group
    columns = res_local // seq_count

    loads = [
        pltpu.make_async_copy(src, dst, load_sem.at[i])
        for i, (src, dst) in enumerate(
            (
                (row_entry_hbm, row_entry),
                (row_exit_hbm, row_exit),
                (col_entry_hbm, col_entry),
                (col_exit_hbm, col_exit),
                (ff_first_hbm, ff_first),
                (ff_second_hbm, ff_second),
            )
        )
    ]
    for load in loads:
        load.start()

    barrier = pltpu.get_barrier_semaphore()

    def greet(axis, me, count):
        def step(k, carry):
            peer = lax.rem(me + k, count)
            pl.semaphore_signal(barrier, inc=1, device_id={axis: peer}, device_id_type=MESH)
            return carry

        lax.fori_loop(1, count, step, 0)

    greet("res", me_res, res_count)
    greet("seq", me_seq, seq_count)

    def send(g, k, src, dst, axis, peer, sem, phase):
        return pltpu.make_async_remote_copy(
            src_ref=src,
            dst_ref=dst,
            send_sem=sem.at[phase, 0, g, k],
            recv_sem=sem.at[phase, 1, g, k],
            device_id={axis: peer},
            device_id_type=MESH,
        )

    def row_copy(g, k):
        peer = lax.rem(me_res + k, res_count)
        return send(g, k, row_sent.at[g, peer], row_in.at[g, me_res], "res", peer, sems, 0)

    def row_return(g, k):
        peer = lax.rem(me_res + k, res_count)
        return send(g, k, row_out.at[g, peer], row_back.at[me_res, g], "res", peer, sems, 1)

    def col_copy(g, k):
        peer = lax.rem(me_seq + k, seq_count)
        return send(
            g, k, col_sent.at[peer * columns + g], col_in.at[g, me_seq], "seq", peer, col_sems, 0
        )

    def col_return(g, k):
        peer = lax.rem(me_seq + k, seq_count)
        return send(
            g, k, col_out.at[g, peer], col_back.at[me_seq * columns + g], "seq", peer, col_sems, 1
        )

    def each(count, act):
        def step(k, carry):
            act(k)
            return carry

        lax.fori_loop(1, count, step, 0)

    for g in range(groups):
        row_sent[g] = standardize(x_ref[:, g], gains[0:1], shifts[0:1])
        if g == 0:
            pl.semaphore_wait(barrier, res_count + seq_count - 2)
        each(res_count, lambda k: row_copy(g, k).start())
        row_in[g, me_res] = row_sent[g, me_res]

    loads[0].wait()
    loads[1].wait()
    turned_value[0] = row_entry[:, 2 * channels : 3 * channels].T
    for g in range(groups):
        each(res_count, lambda k: row_copy(g, k).wait_recv())
        for i in range(group):
            result = attend(
                row_in[g, :, i].reshape(res_count * res_local, channels),
                row_entry,
                turned_value[0],
                row_gate[...],
                row_exit[...],
                mixed_row,
            )
            row_out[g, :, i] = result.astype(BF16).reshape(res_count, res_local, channels)
        each(res_count, lambda k: row_return(g, k).start())
        row_back[me_res, g] = row_out[g, me_res]

    loads[2].wait()
    loads[3].wait()
    turned_value[1] = col_entry[:, 2 * channels : 3 * channels].T
    for g in range(groups):
        each(res_count, lambda k: row_return(g, k).wait_recv())
        for source in range(res_count):
            first = source * items + g * group
            after_row[first : first + group] = (
                x_ref[source, g] + row_back[source, g].astype(F32) + row_shift[...]
            )

    for g in range(columns):
        for part in range(seq_count):
            j = part * columns + g
            here = after_row[:, j, :]
            after_turned[j] = here
            col_sent[j] = standardize(here, gains[1:2], shifts[1:2])
        each(seq_count, lambda k: col_copy(g, k).start())
        col_in[g, me_seq] = col_sent[me_seq * columns + g]

    for g in range(columns):
        each(seq_count, lambda k: col_copy(g, k).wait_recv())
        result = attend(
            col_in[g].reshape(seq_count * seq_local, channels),
            col_entry,
            turned_value[1],
            col_gate[...],
            col_exit[...],
            mixed_col,
        )
        col_out[g] = result.astype(BF16).reshape(seq_count, seq_local, channels)
        each(seq_count, lambda k: col_return(g, k).start())
        col_back[me_seq * columns + g] = col_out[g, me_seq]

    loads[4].wait()
    loads[5].wait()
    for g in range(columns):
        each(seq_count, lambda k: col_return(g, k).wait_recv())
        places = [part * columns + g for part in range(seq_count)]
        done = jnp.concatenate(
            [after_turned[j] + col_back[j].astype(F32) for j in places], axis=0
        ) + col_shift[...]
        normed = standardize(done, gains[2:3], shifts[2:3])
        inner = jnp.maximum(dot(normed, ff_first[...]) + ff_first_shift[...], 0.0).astype(BF16)
        final = done + dot(inner, ff_second[...]) + ff_second_shift[...]
        for part, j in enumerate(places):
            out_ref[:, j, :] = final[part * seq_local : (part + 1) * seq_local]

    for g in range(groups):
        each(res_count, lambda k: row_copy(g, k).wait_send())
        each(res_count, lambda k: row_return(g, k).wait_send())
    for g in range(columns):
        each(seq_count, lambda k: col_copy(g, k).wait_send())
        each(seq_count, lambda k: col_return(g, k).wait_send())


def shards(
    alignment_tensor,
    standardizer_factors,
    standardizer_offsets,
    horizontal_entry_matrix,
    horizontal_sigmoid_offset,
    horizontal_exit_matrix,
    horizontal_exit_offset,
    vertical_entry_matrix,
    vertical_sigmoid_offset,
    vertical_exit_matrix,
    vertical_exit_offset,
    feedforward_first_matrix,
    feedforward_first_offset,
    feedforward_second_matrix,
    feedforward_second_offset,
):
    seq_local, res_local, channels = alignment_tensor.shape
    hidden = feedforward_first_matrix.shape[1]
    res_count = lax.axis_size("res")
    seq_count = lax.axis_size("seq")
    items = seq_local // res_count
    group = 2 if items % 2 == 0 else 1
    groups = items // group
    columns = res_local // seq_count
    vmem = pl.BlockSpec(memory_space=pltpu.VMEM)
    anywhere = pl.BlockSpec(memory_space=pl.ANY)
    row_length, col_length = res_local * res_count, seq_local * seq_count

    def line(vector):
        return vector.reshape(1, -1)

    def mixed(length):
        rows = channels if length > 256 else 16
        wide = length if length > 256 else 128
        return [pltpu.VMEM((rows, wide), BF16), pltpu.VMEM((rows, wide), F32)]

    tokens = seq_local * res_local
    return pl.pallas_call(
        functools.partial(block, res_count, seq_count),
        out_shape=jax.ShapeDtypeStruct(alignment_tensor.shape, F32),
        in_specs=[vmem] * 9 + [anywhere] * 6,
        out_specs=vmem,
        scratch_shapes=[
            pltpu.VMEM(horizontal_entry_matrix.shape, BF16),
            pltpu.VMEM(horizontal_exit_matrix.shape, BF16),
            pltpu.VMEM(vertical_entry_matrix.shape, BF16),
            pltpu.VMEM(vertical_exit_matrix.shape, BF16),
            pltpu.VMEM(feedforward_first_matrix.shape, BF16),
            pltpu.VMEM(feedforward_second_matrix.shape, BF16),
            pltpu.VMEM((2, channels, channels), BF16),
            pltpu.VMEM((groups, res_count, group, res_local, channels), BF16),
            pltpu.VMEM((groups, res_count, group, res_local, channels), BF16),
            pltpu.VMEM((groups, res_count, group, res_local, channels), BF16),
            pltpu.VMEM((res_count, groups, group, res_local, channels), BF16),
            pltpu.VMEM((seq_local, res_local, channels), F32),
            pltpu.VMEM((res_local, seq_local, channels), F32),
            pltpu.VMEM((res_local, seq_local, channels), BF16),
            pltpu.VMEM((columns, seq_count, seq_local, channels), BF16),
            pltpu.VMEM((columns, seq_count, seq_local, channels), BF16),
            pltpu.VMEM((res_local, seq_local, channels), BF16),
            mixed(row_length),
            mixed(col_length),
            pltpu.SemaphoreType.DMA((6,)),
            pltpu.SemaphoreType.DMA((2, 2, groups, res_count)),
            pltpu.SemaphoreType.DMA((2, 2, columns, seq_count)),
        ],
        compiler_params=pltpu.CompilerParams(
            collective_id=0, has_side_effects=True, vmem_limit_bytes=48 * 1024 * 1024
        ),
        cost_estimate=pl.CostEstimate(
            flops=2 * tokens * channels * (10 * channels + 2 * hidden),
            bytes_accessed=16 * tokens * channels,
            transcendentals=tokens * HEADS * (row_length + col_length),
        ),
    )(
        alignment_tensor.reshape(res_count, groups, group, res_local, channels),
        standardizer_factors,
        standardizer_offsets,
        line(horizontal_sigmoid_offset),
        line(horizontal_exit_offset),
        line(vertical_sigmoid_offset),
        line(vertical_exit_offset),
        line(feedforward_first_offset),
        line(feedforward_second_offset),
        horizontal_entry_matrix,
        horizontal_exit_matrix,
        vertical_entry_matrix,
        vertical_exit_matrix,
        feedforward_first_matrix,
        feedforward_second_matrix,
    )


def solution(mesh):
    return jax.shard_map(
        shards,
        mesh=mesh,
        in_specs=(P("seq", "res", None),) + (P(),) * 14,
        out_specs=P("seq", "res", None),
        check_vma=False,
    )
```

profile of v0, /device:TPU:0, one launch (start us, length us, event | category | flops | bytes accessed | tf_op | source)
XLA Modules:
  0.0 53.6 jit_solution(5417623269550911670)
XLA Ops:
  0.0 0.0 copy-start.9
  0.0 0.0 copy-start.8
  0.0 0.0 copy-start.7
  0.0 0.0 copy-start.10
  0.0 0.7 %copy-done.9 = f32[1024]{0:T(1024)S(1)} copy-done((f32[1024]{0:T(1024)S(1)}, f32[1024]{0:T(1024)}, u32[]{:S(2)}) %copy-start.9) | copy-done | bytes 4120
  0.7 0.0 copy-done.8
  0.7 0.0 copy-done.7
  0.7 0.0 copy-done.10
  0.7 0.0 copy-start
  0.7 1.1 %copy-done = f32[48,16,256]{2,1,0:T(8,128)S(1)} copy-done((f32[48,16,256]{2,1,0:T(8,128)S(1)}, f32[48,16,256]{2,1,0:T(8,128)}, u32[]{:S(2)}) %copy-start) | copy-done | bytes 786456
  1.9 0.0 copy-start.1
  1.9 1.0 %copy-done.1 = bf16[256,1024]{1,0:T(8,128)(2,1)S(1)} copy-done((bf16[256,1024]{1,0:T(8,128)(2,1)S(1)}, bf16[256,1024]{1,0:T(8,128)(2,1)}, u32[]{:S(2)}) %copy-start.1) | copy-done | bytes 524312
  2.9 0.0 copy-start.2
  2.9 1.0 %copy-done.2 = bf16[256,1024]{1,0:T(8,128)(2,1)S(1)} copy-done((bf16[256,1024]{1,0:T(8,128)(2,1)S(1)}, bf16[256,1024]{1,0:T(8,128)(2,1)}, u32[]{:S(2)}) %copy-start.2) | copy-done | bytes 524312
  3.9 1.0 %copy-done.3 = bf16[256,1024]{1,0:T(8,128)(2,1)S(1)} copy-done((bf16[256,1024]{1,0:T(8,128)(2,1)S(1)}, bf16[256,1024]{1,0:T(8,128)(2,1)}, u32[]{:S(2)}) %copy-start.3) | copy-done | bytes 524312
  5.0 1.0 %copy-done.4 = bf16[1024,256]{1,0:T(8,128)(2,1)S(1)} copy-done((bf16[1024,256]{1,0:T(8,128)(2,1)S(1)}, bf16[1024,256]{1,0:T(8,128)(2,1)}, u32[]{:S(2)}) %copy-start.4) | copy-done | bytes 524312
  6.0 0.9 %copy-done.5 = bf16[256,256]{1,0:T(8,128)(2,1)S(1)} copy-done((bf16[256,256]{1,0:T(8,128)(2,1)S(1)}, bf16[256,256]{1,0:T(8,128)(2,1)}, u32[]{:S(2)}) %copy-start.5) | copy-done | bytes 131096
  6.9 0.9 %copy-done.6 = bf16[256,256]{1,0:T(8,128)(2,1)S(1)} copy-done((bf16[256,256]{1,0:T(8,128)(2,1)S(1)}, bf16[256,256]{1,0:T(8,128)(2,1)}, u32[]{:S(2)}) %copy-start.6) | copy-done | bytes 131096
  7.8 0.7 %copy-done.11 = f32[256]{0:T(256)S(1)} copy-done((f32[256]{0:T(256)S(1)}, f32[256]{0:T(256)}, u32[]{:S(2)}) %copy-start.11) | copy-done | bytes 1048
  8.5 0.7 %copy-done.12 = f32[256]{0:T(256)S(1)} copy-done((f32[256]{0:T(256)S(1)}, f32[256]{0:T(256)}, u32[]{:S(2)}) %copy-start.12) | copy-done | bytes 1048
  9.2 0.7 %copy-done.13 = f32[256]{0:T(256)S(1)} copy-done((f32[256]{0:T(256)S(1)}, f32[256]{0:T(256)}, u32[]{:S(2)}) %copy-start.13) | copy-done | bytes 1048
  9.9 0.7 %copy-done.14 = f32[256]{0:T(256)S(1)} copy-done((f32[256]{0:T(256)S(1)}, f32[256]{0:T(256)}, u32[]{:S(2)}) %copy-start.14) | copy-done | bytes 1048
  10.6 42.1 %shard_map.145 = f32[48,16,256]{2,1,0:T(8,128)S(1)} custom-call(f32[8,3,2,16,256]{4,3,2,1,0:T(8,128)S(1)} %bitcast.7, f32[3,256]{1,0:T(4,128)S(1)} %copy-done.7, f32[3,256]{1,0:T(4,128)S(1)} %copy-done.8, f32[1,256]{1,0:T(1,128)S(1)} %bitcast.9, f32[1,256]{1,0:T(1,128)S(1)} %bitcast.10, f32[1,256]{1,0:T(1,128)S(1)} %bitcast.11, f32[1,256]{1,0:T(1,128)S(1)} %bitcast.12, ...), custom_call_target="tpu_custom_call" | custom-call | flops 1811939328 | bytes 3145728 | tf_op jit(solution)/shard_map/pallas_call | solution.py:302
  52.7 0.9 %copy.17 = f32[48,16,256]{2,1,0:T(8,128)} copy(f32[48,16,256]{2,1,0:T(8,128)S(1)} %shard_map.145) | data formatting | bytes 1572864
  (8 shorter events, 0.0 us)
Async XLA Ops:
  0.0 0.7 %copy-start.9 = (f32[1024]{0:T(1024)S(1)}, f32[1024]{0:T(1024)}, u32[]{:S(2)}) copy-start(f32[1024]{0:T(1024)} %param.27) | copy-start | bytes 12292
  0.0 0.7 %copy-start.8 = (f32[3,256]{1,0:T(4,128)S(1)}, f32[3,256]{1,0:T(4,128)}, u32[]{:S(2)}) copy-start(f32[3,256]{1,0:T(4,128)} %shifts.1) | copy-start | bytes 9220
  0.0 0.7 %copy-start.7 = (f32[3,256]{1,0:T(4,128)S(1)}, f32[3,256]{1,0:T(4,128)}, u32[]{:S(2)}) copy-start(f32[3,256]{1,0:T(4,128)} %gains.1) | copy-start | bytes 9220
  0.0 0.7 %copy-start.10 = (f32[256]{0:T(256)S(1)}, f32[256]{0:T(256)}, u32[]{:S(2)}) copy-start(f32[256]{0:T(256)} %param.19) | copy-start | bytes 3076
  0.7 1.1 %copy-start = (f32[48,16,256]{2,1,0:T(8,128)S(1)}, f32[48,16,256]{2,1,0:T(8,128)}, u32[]{:S(2)}) copy-start(f32[48,16,256]{2,1,0:T(8,128)} %param.15) | copy-start | bytes 2359300
  1.9 1.0 %copy-start.1 = (bf16[256,1024]{1,0:T(8,128)(2,1)S(1)}, bf16[256,1024]{1,0:T(8,128)(2,1)}, u32[]{:S(2)}) copy-start(bf16[256,1024]{1,0:T(8,128)(2,1)} %row_entry_hbm.1) | copy-start | bytes 1572868
  2.9 1.0 %copy-start.2 = (bf16[256,1024]{1,0:T(8,128)(2,1)S(1)}, bf16[256,1024]{1,0:T(8,128)(2,1)}, u32[]{:S(2)}) copy-start(bf16[256,1024]{1,0:T(8,128)(2,1)} %col_entry_hbm.1) | copy-start | bytes 1572868
  3.9 1.0 %copy-start.3 = (bf16[256,1024]{1,0:T(8,128)(2,1)S(1)}, bf16[256,1024]{1,0:T(8,128)(2,1)}, u32[]{:S(2)}) copy-start(bf16[256,1024]{1,0:T(8,128)(2,1)} %ff_first_hbm.1) | copy-start | bytes 1572868
  5.0 1.0 %copy-start.4 = (bf16[1024,256]{1,0:T(8,128)(2,1)S(1)}, bf16[1024,256]{1,0:T(8,128)(2,1)}, u32[]{:S(2)}) copy-start(bf16[1024,256]{1,0:T(8,128)(2,1)} %ff_second_hbm.1) | copy-start | bytes 1572868
  6.0 0.9 %copy-start.5 = (bf16[256,256]{1,0:T(8,128)(2,1)S(1)}, bf16[256,256]{1,0:T(8,128)(2,1)}, u32[]{:S(2)}) copy-start(bf16[256,256]{1,0:T(8,128)(2,1)} %row_exit_hbm.1) | copy-start | bytes 393220
  6.9 0.9 %copy-start.6 = (bf16[256,256]{1,0:T(8,128)(2,1)S(1)}, bf16[256,256]{1,0:T(8,128)(2,1)}, u32[]{:S(2)}) copy-start(bf16[256,256]{1,0:T(8,128)(2,1)} %col_exit_hbm.1) | copy-start | bytes 393220
  7.8 0.7 %copy-start.11 = (f32[256]{0:T(256)S(1)}, f32[256]{0:T(256)}, u32[]{:S(2)}) copy-start(f32[256]{0:T(256)} %param.21) | copy-start | bytes 3076
  8.5 0.7 %copy-start.12 = (f32[256]{0:T(256)S(1)}, f32[256]{0:T(256)}, u32[]{:S(2)}) copy-start(f32[256]{0:T(256)} %param.23) | copy-start | bytes 3076
  9.2 0.7 %copy-start.13 = (f32[256]{0:T(256)S(1)}, f32[256]{0:T(256)}, u32[]{:S(2)}) copy-start(f32[256]{0:T(256)} %param.25) | copy-start | bytes 3076
  9.9 0.7 %copy-start.14 = (f32[256]{0:T(256)S(1)}, f32[256]{0:T(256)}, u32[]{:S(2)}) copy-start(f32[256]{0:T(256)} %param.29) | copy-start | bytes 3076
where the time goes:
time: 54.1 us; the launch traced here: 53.6 us
  Pallas kernels  42.1 us (78%)
  local copies, waits for them, and re-layouts  11.4 us (21%)
    pallas_call x1, Pallas kernels, shards(): pl.pallas_call(functools.partial(block, res_count, seq_count), out_shape=...  42.1 us
    unnamed x31, local copies, waits for them, and re-layouts  11.4 us

commit v1 on v0

--- a/solution.py
+++ b/solution.py
@@ -29,44 +29,81 @@
     return lax.dot_general(left, right, (((1,), (1,)), ((), ())), preferred_element_type=F32)
 
 
-def attend(normed, entry, value_turned, gate_offset, exit_matrix, mixed):
-    length, channels = normed.shape
+def attend(normed, length, entry, value_turned, gate_offset, exit_matrix, mixed):
+    channels = normed.shape[1]
     size = channels // HEADS
+    count = normed.shape[0] // length
     query = (dot(normed, entry[:, :channels]) * size ** (-0.5)).astype(BF16)
     key = dot(normed, entry[:, channels : 2 * channels]).astype(BF16)
-    value = dot_nt(value_turned, normed).astype(BF16)
     gate = jax.nn.sigmoid(dot(normed, entry[:, 3 * channels :]) + gate_offset)
+    spans = [slice(n * length, (n + 1) * length) for n in range(count)]
+    values = [dot_nt(value_turned, normed[span]).astype(BF16) for span in spans]
     lane = lax.broadcasted_iota(jnp.int32, (1, channels), 1)
 
-    def one_head(head, own_values):
+    def mask(head):
         low = head * size
-        mask = jnp.where((lane >= low) & (lane < low + size), 1.0, 0.0).astype(BF16)
-        scores = dot_nt(key * mask, query)
-        weights = jnp.exp(scores - jnp.max(scores, axis=0, keepdims=True))
-        total = jnp.sum(weights, axis=0, keepdims=True)
-        return dot(own_values, weights.astype(BF16)) / total
+        return jnp.where((lane >= low) & (lane < low + size), 1.0, 0.0).astype(BF16)
 
     if length <= 256:
-        outs = [one_head(h, value[h * size : (h + 1) * size]) for h in range(HEADS)]
-        turned = jnp.concatenate(outs, axis=0)
+        masks = [mask(head) for head in range(HEADS)]
+        scores = [
+            dot_nt(jnp.concatenate([key[span] * m for m in masks], axis=0), query[span])
+            for span in spans
+        ]
+        heads = [
+            (value[h * size : (h + 1) * size], score[h * length : (h + 1) * length])
+            for value, score in zip(values, scores)
+            for h in range(HEADS)
+        ]
+        peaks = [jnp.max(score, axis=0, keepdims=True) for _, score in heads]
+        weights = [jnp.exp(score - peak) for (_, score), peak in zip(heads, peaks)]
+        totals = [jnp.sum(weight, axis=0, keepdims=True) for weight in weights]
+        outs = [
+            dot(value, weight.astype(BF16)) / total
+            for (value, _), weight, total in zip(heads, weights, totals)
+        ]
+        turned = [
+            jnp.concatenate(outs[n * HEADS : (n + 1) * HEADS], axis=0).T for n in range(count)
+        ]
     else:
         held, out = mixed
-        held[...] = value
-
-        def step(head, carry):
-            rows = pl.ds(pl.multiple_of(head * size, size), size)
-            out[rows, :] = one_head(head, held[rows, :])
-            return carry
-
-        lax.fori_loop(0, HEADS, step, 0)
-        turned = out[...]
-    gated = (gate * turned.T).astype(BF16)
+        turned = []
+        for span, value in zip(spans, values):
+            held[...] = value
+
+            def step(head, carry):
+                rows = pl.ds(pl.multiple_of(head * size, size), size)
+                score = dot_nt(key[span] * mask(head), query[span])
+                weight = jnp.exp(score - jnp.max(score, axis=0, keepdims=True))
+                total = jnp.sum(weight, axis=0, keepdims=True)
+                out[rows, :] = dot(held[rows, :], weight.astype(BF16)) / total
+                return carry
+
+            lax.fori_loop(0, HEADS, step, 0)
+            turned.append(out[...].T)
+    gated = (gate * jnp.concatenate(turned, axis=0)).astype(BF16)
     return dot(gated, exit_matrix)
 
 
 def block(
     res_count,
     seq_count,
+    x_hbm,
+    gains_hbm,
+    shifts_hbm,
+    row_gate_hbm,
+    row_shift_hbm,
+    col_gate_hbm,
+    col_shift_hbm,
+    ff_first_shift_hbm,
+    ff_second_shift_hbm,
+    row_entry_hbm,
+    row_exit_hbm,
+    col_entry_hbm,
+    col_exit_hbm,
+    ff_first_hbm,
+    ff_second_hbm,
+    out_ref,
     x_ref,
     gains,
     shifts,
@@ -76,13 +113,6 @@
     col_shift,
     ff_first_shift,
     ff_second_shift,
-    row_entry_hbm,
-    row_exit_hbm,
-    col_entry_hbm,
-    col_exit_hbm,
-    ff_first_hbm,
-    ff_second_hbm,
-    out_ref,
     row_entry,
     row_exit,
     col_entry,
@@ -102,6 +132,7 @@
     col_back,
     mixed_row,
     mixed_col,
+    x_sem,
     load_sem,
     sems,
     col_sems,
@@ -112,23 +143,8 @@
     res_local, channels = x_ref.shape[3], x_ref.shape[4]
     seq_local = after_row.shape[0]
     items = groups * group
+    row_length = res_count * res_local
     columns = res_local // seq_count
-
-    loads = [
-        pltpu.make_async_copy(src, dst, load_sem.at[i])
-        for i, (src, dst) in enumerate(
-            (
-                (row_entry_hbm, row_entry),
-                (row_exit_hbm, row_exit),
-                (col_entry_hbm, col_entry),
-                (col_exit_hbm, col_exit),
-                (ff_first_hbm, ff_first),
-                (ff_second_hbm, ff_second),
-            )
-        )
-    ]
-    for load in loads:
-        load.start()
 
     barrier = pltpu.get_barrier_semaphore()
 
@@ -142,6 +158,31 @@
 
     greet("res", me_res, res_count)
     greet("seq", me_seq, seq_count)
+
+    x_loads = [
+        pltpu.make_async_copy(x_hbm.at[:, g], x_ref.at[:, g], x_sem.at[g]) for g in range(groups)
+    ]
+    pairs = (
+        (gains_hbm, gains),
+        (shifts_hbm, shifts),
+        (row_gate_hbm, row_gate),
+        (row_shift_hbm, row_shift),
+        (col_gate_hbm, col_gate),
+        (col_shift_hbm, col_shift),
+        (ff_first_shift_hbm, ff_first_shift),
+        (ff_second_shift_hbm, ff_second_shift),
+        (row_entry_hbm, row_entry),
+        (row_exit_hbm, row_exit),
+        (col_entry_hbm, col_entry),
+        (col_exit_hbm, col_exit),
+        (ff_first_hbm, ff_first),
+        (ff_second_hbm, ff_second),
+    )
+    loads = [
+        pltpu.make_async_copy(src, dst, load_sem.at[i]) for i, (src, dst) in enumerate(pairs)
+    ]
+    for load in loads[:2] + x_loads + loads[2:]:
+        load.start()
 
     def send(g, k, src, dst, axis, peer, sem, phase):
         return pltpu.make_async_remote_copy(
@@ -180,33 +221,41 @@
 
         lax.fori_loop(1, count, step, 0)
 
+    loads[0].wait()
+    loads[1].wait()
     for g in range(groups):
+        x_loads[g].wait()
         row_sent[g] = standardize(x_ref[:, g], gains[0:1], shifts[0:1])
         if g == 0:
             pl.semaphore_wait(barrier, res_count + seq_count - 2)
         each(res_count, lambda k: row_copy(g, k).start())
         row_in[g, me_res] = row_sent[g, me_res]
 
-    loads[0].wait()
-    loads[1].wait()
+    for i in (2, 3, 8, 9):
+        loads[i].wait()
     turned_value[0] = row_entry[:, 2 * channels : 3 * channels].T
     for g in range(groups):
         each(res_count, lambda k: row_copy(g, k).wait_recv())
+        result = attend(
+            jnp.concatenate(
+                [row_in[g, :, i].reshape(row_length, channels) for i in range(group)], axis=0
+            ),
+            row_length,
+            row_entry,
+            turned_value[0],
+            row_gate[...],
+            row_exit[...],
+            mixed_row,
+        ).astype(BF16)
         for i in range(group):
-            result = attend(
-                row_in[g, :, i].reshape(res_count * res_local, channels),
-                row_entry,
-                turned_value[0],
-                row_gate[...],
-                row_exit[...],
-                mixed_row,
+            row_out[g, :, i] = result[i * row_length : (i + 1) * row_length].reshape(
+                res_count, res_local, channels
             )
-            row_out[g, :, i] = result.astype(BF16).reshape(res_count, res_local, channels)
         each(res_count, lambda k: row_return(g, k).start())
         row_back[me_res, g] = row_out[g, me_res]
 
-    loads[2].wait()
-    loads[3].wait()
+    for i in (4, 5, 10, 11):
+        loads[i].wait()
     turned_value[1] = col_entry[:, 2 * channels : 3 * channels].T
     for g in range(groups):
         each(res_count, lambda k: row_return(g, k).wait_recv())
@@ -229,6 +278,7 @@
         each(seq_count, lambda k: col_copy(g, k).wait_recv())
         result = attend(
             col_in[g].reshape(seq_count * seq_local, channels),
+            seq_count * seq_local,
             col_entry,
             turned_value[1],
             col_gate[...],
@@ -239,8 +289,8 @@
         each(seq_count, lambda k: col_return(g, k).start())
         col_back[me_seq * columns + g] = col_out[g, me_seq]
 
-    loads[4].wait()
-    loads[5].wait()
+    for i in (6, 7, 12, 13):
+        loads[i].wait()
     for g in range(columns):
         each(seq_count, lambda k: col_return(g, k).wait_recv())
         places = [part * columns + g for part in range(seq_count)]
@@ -287,7 +337,7 @@
     groups = items // group
     columns = res_local // seq_count
     vmem = pl.BlockSpec(memory_space=pltpu.VMEM)
-    anywhere = pl.BlockSpec(memory_space=pl.ANY)
+    in_hbm = pl.BlockSpec(memory_space=pltpu.HBM)
     row_length, col_length = res_local * res_count, seq_local * seq_count
 
     def line(vector):
@@ -302,9 +352,18 @@
     return pl.pallas_call(
         functools.partial(block, res_count, seq_count),
         out_shape=jax.ShapeDtypeStruct(alignment_tensor.shape, F32),
-        in_specs=[vmem] * 9 + [anywhere] * 6,
+        in_specs=[in_hbm] * 15,
         out_specs=vmem,
         scratch_shapes=[
+            pltpu.VMEM((res_count, groups, group, res_local, channels), F32),
+            pltpu.VMEM(standardizer_factors.shape, F32),
+            pltpu.VMEM(standardizer_offsets.shape, F32),
+            pltpu.VMEM((1, channels), F32),
+            pltpu.VMEM((1, channels), F32),
+            pltpu.VMEM((1, channels), F32),
+            pltpu.VMEM((1, channels), F32),
+            pltpu.VMEM((1, hidden), F32),
+            pltpu.VMEM((1, channels), F32),
             pltpu.VMEM(horizontal_entry_matrix.shape, BF16),
             pltpu.VMEM(horizontal_exit_matrix.shape, BF16),
             pltpu.VMEM(vertical_entry_matrix.shape, BF16),
@@ -324,12 +383,13 @@
             pltpu.VMEM((res_local, seq_local, channels), BF16),
             mixed(row_length),
             mixed(col_length),
-            pltpu.SemaphoreType.DMA((6,)),
+            pltpu.SemaphoreType.DMA((groups,)),
+            pltpu.SemaphoreType.DMA((14,)),
             pltpu.SemaphoreType.DMA((2, 2, groups, res_count)),
             pltpu.SemaphoreType.DMA((2, 2, columns, seq_count)),
         ],
         compiler_params=pltpu.CompilerParams(
-            collective_id=0, has_side_effects=True, vmem_limit_bytes=48 * 1024 * 1024
+            collective_id=0, has_side_effects=True, vmem_limit_bytes=63 * 1024 * 1024
         ),
         cost_estimate=pl.CostEstimate(
             flops=2 * tokens * channels * (10 * channels + 2 * hidden),

time: 54.1 us -> 41.4 us (0.77)
  local copies, waits for them, and re-layouts: 11.4 us -> 2.06 us
  Pallas kernels: 42.1 us -> 39.2 us
    unnamed x31 -> x1, local copies, waits for them, and re-layouts: 11.4 us -> 2.06 us
    pallas_call x1, Pallas kernels: 42.1 us -> 39.2 us  [shards(): pl.pallas_call(functools.partial(block, res_count, seq_count), out_shape=...]
where the time goes in v1:
time: 41.4 us; the launch traced here: 41.3 us
  Pallas kernels  39.2 us (95%)
  local copies, waits for them, and re-layouts  2.06 us (5%)
    pallas_call x1, Pallas kernels, shards(): pl.pallas_call(functools.partial(block, res_count, seq_count), out_shape=...  39.2 us
    unnamed x1, local copies, waits for them, and re-layouts  2.06 us

profile of v1, /device:TPU:0, one launch (start us, length us, event | category | flops | bytes accessed | tf_op | source)
XLA Modules:
  0.0 41.3 jit_solution(3713539300735790685)
XLA Ops:
  0.0 39.2 %shard_map.145 = f32[48,16,256]{2,1,0:T(8,128)} custom-call(f32[8,3,2,16,256]{4,3,2,1,0:T(8,128)} %bitcast.7, f32[3,256]{1,0:T(4,128)} %gains_hbm.1, f32[3,256]{1,0:T(4,128)} %shifts_hbm.1, f32[1,256]{1,0:T(1,128)} %bitcast.9, f32[1,256]{1,0:T(1,128)} %bitcast.10, f32[1,256]{1,0:T(1,128)} %bitcast.11, f32[1,256]{1,0:T(1,128)} %bitcast.12, ...), custom_call_target="tpu_custom_call" | custom-call | flops 1811939328 | bytes 3145728 | tf_op jit(solution)/shard_map/pallas_call | solution.py:352
  39.2 2.1 %copy.17 = f32[48,16,256]{2,1,0:T(8,128)} copy(f32[48,16,256]{2,1,0:T(8,128)} %shard_map.145) | data formatting | bytes 1572864

commit v2 on v1

--- a/solution.py
+++ b/solution.py
@@ -37,8 +37,17 @@
     key = dot(normed, entry[:, channels : 2 * channels]).astype(BF16)
     gate = jax.nn.sigmoid(dot(normed, entry[:, 3 * channels :]) + gate_offset)
     spans = [slice(n * length, (n + 1) * length) for n in range(count)]
-    values = [dot_nt(value_turned, normed[span]).astype(BF16) for span in spans]
+    value = dot_nt(value_turned, normed).astype(BF16)
+    values = [value[:, span] for span in spans]
+    ones = jnp.ones((16, length), BF16)
     lane = lax.broadcasted_iota(jnp.int32, (1, channels), 1)
+
+    def weigh(score, value):
+        weight = jnp.exp((score - jnp.max(score, axis=0, keepdims=True)).astype(BF16))
+        return dot(jnp.concatenate([value, ones], axis=0), weight)
+
+    def share(product):
+        return product[:size] * (1.0 / product[size : size + 1])
 
     def mask(head):
         low = head * size
@@ -55,13 +64,7 @@
             for value, score in zip(values, scores)
             for h in range(HEADS)
         ]
-        peaks = [jnp.max(score, axis=0, keepdims=True) for _, score in heads]
-        weights = [jnp.exp(score - peak) for (_, score), peak in zip(heads, peaks)]
-        totals = [jnp.sum(weight, axis=0, keepdims=True) for weight in weights]
-        outs = [
-            dot(value, weight.astype(BF16)) / total
-            for (value, _), weight, total in zip(heads, weights, totals)
-        ]
+        outs = [share(product) for product in [weigh(score, value) for value, score in heads]]
         turned = [
             jnp.concatenate(outs[n * HEADS : (n + 1) * HEADS], axis=0).T for n in range(count)
         ]
@@ -74,9 +77,7 @@
             def step(head, carry):
                 rows = pl.ds(pl.multiple_of(head * size, size), size)
                 score = dot_nt(key[span] * mask(head), query[span])
-                weight = jnp.exp(score - jnp.max(score, axis=0, keepdims=True))
-                total = jnp.sum(weight, axis=0, keepdims=True)
-                out[rows, :] = dot(held[rows, :], weight.astype(BF16)) / total
+                out[rows, :] = share(weigh(score, held[rows, :]))
                 return carry
 
             lax.fori_loop(0, HEADS, step, 0)

time: 41.4 us -> 41.4 us (level)
  no operation moved by 1% of the time
where the time goes in v2:
time: 41.4 us; the launch traced here: 41.2 us
  Pallas kernels  39.2 us (95%)
  local copies, waits for them, and re-layouts  2.06 us (5%)
    pallas_call x1, Pallas kernels, shards(): pl.pallas_call(functools.partial(block, res_count, seq_count), out_shape=...  39.2 us
    unnamed x1, local copies, waits for them, and re-layouts  2.06 us

profile of v2, /device:TPU:0, one launch (start us, length us, event | category | flops | bytes accessed | tf_op | source)
XLA Modules:
  0.0 41.2 jit_solution(18188604831099576479)
XLA Ops:
  0.0 39.2 %shard_map.145 = f32[48,16,256]{2,1,0:T(8,128)} custom-call(f32[8,3,2,16,256]{4,3,2,1,0:T(8,128)} %bitcast.7, f32[3,256]{1,0:T(4,128)} %gains_hbm.1, f32[3,256]{1,0:T(4,128)} %shifts_hbm.1, f32[1,256]{1,0:T(1,128)} %bitcast.9, f32[1,256]{1,0:T(1,128)} %bitcast.10, f32[1,256]{1,0:T(1,128)} %bitcast.11, f32[1,256]{1,0:T(1,128)} %bitcast.12, ...), custom_call_target="tpu_custom_call" | custom-call | flops 1811939328 | bytes 3145728 | tf_op jit(solution)/shard_map/pallas_call | solution.py:353
  39.2 2.1 %copy.17 = f32[48,16,256]{2,1,0:T(8,128)} copy(f32[48,16,256]{2,1,0:T(8,128)} %shard_map.145) | data formatting | bytes 1572864

commit v3 on v2

--- a/solution.py
+++ b/solution.py
@@ -136,6 +136,7 @@
     x_sem,
     load_sem,
     sems,
+    back_sems,
     col_sems,
 ):
     me_res = lax.axis_index("res")
@@ -146,6 +147,8 @@
     items = groups * group
     row_length = res_count * res_local
     columns = res_local // seq_count
+    halves = row_out.shape[0]
+    part_rows, part_columns = res_local // halves, columns // halves
 
     barrier = pltpu.get_barrier_semaphore()
 
@@ -199,20 +202,29 @@
         peer = lax.rem(me_res + k, res_count)
         return send(g, k, row_sent.at[g, peer], row_in.at[g, me_res], "res", peer, sems, 0)
 
-    def row_return(g, k):
+    def row_return(h, g, k):
         peer = lax.rem(me_res + k, res_count)
-        return send(g, k, row_out.at[g, peer], row_back.at[me_res, g], "res", peer, sems, 1)
+        return send(
+            h * groups + g,
+            k,
+            row_out.at[h, g, peer],
+            row_back.at[h, me_res, g],
+            "res",
+            peer,
+            back_sems,
+            0,
+        )
 
     def col_copy(g, k):
         peer = lax.rem(me_seq + k, seq_count)
         return send(
-            g, k, col_sent.at[peer * columns + g], col_in.at[g, me_seq], "seq", peer, col_sems, 0
+            g, k, col_sent.at[g, peer], col_in.at[g, me_seq], "seq", peer, col_sems, 0
         )
 
     def col_return(g, k):
         peer = lax.rem(me_seq + k, seq_count)
         return send(
-            g, k, col_out.at[g, peer], col_back.at[me_seq * columns + g], "seq", peer, col_sems, 1
+            g, k, col_out.at[g, peer], col_back.at[g, me_seq], "seq", peer, col_sems, 1
         )
 
     def each(count, act):
@@ -247,35 +259,44 @@
             row_gate[...],
             row_exit[...],
             mixed_row,
-        ).astype(BF16)
-        for i in range(group):
-            row_out[g, :, i] = result[i * row_length : (i + 1) * row_length].reshape(
-                res_count, res_local, channels
-            )
-        each(res_count, lambda k: row_return(g, k).start())
-        row_back[me_res, g] = row_out[g, me_res]
+        )
+        result = result.reshape(group, res_count, res_local, channels)
+        for h in range(halves):
+            rows = slice(h * part_rows, (h + 1) * part_rows)
+            row_out[h, g] = jnp.concatenate(
+                [result[i, :, rows] for i in range(group)], axis=1
+            ).astype(BF16)
+        each(res_count, lambda k: row_return(0, g, k).start())
+        for h in range(1, halves):
+            if g > 0:
+                each(res_count, lambda k: row_return(h, g - 1, k).start())
+            if g == groups - 1:
+                each(res_count, lambda k: row_return(h, g, k).start())
+        for h in range(halves):
+            row_back[h, me_res, g] = row_out[h, g, me_res]
 
     for i in (4, 5, 10, 11):
         loads[i].wait()
     turned_value[1] = col_entry[:, 2 * channels : 3 * channels].T
-    for g in range(groups):
-        each(res_count, lambda k: row_return(g, k).wait_recv())
-        for source in range(res_count):
-            first = source * items + g * group
-            after_row[first : first + group] = (
-                x_ref[source, g] + row_back[source, g].astype(F32) + row_shift[...]
-            )
-
-    for g in range(columns):
-        for part in range(seq_count):
-            j = part * columns + g
-            here = after_row[:, j, :]
-            after_turned[j] = here
-            col_sent[j] = standardize(here, gains[1:2], shifts[1:2])
-        each(seq_count, lambda k: col_copy(g, k).start())
-        col_in[g, me_seq] = col_sent[me_seq * columns + g]
-
-    for g in range(columns):
+    def send_columns(h):
+        rows = slice(h * part_rows, (h + 1) * part_rows)
+        for g in range(groups):
+            each(res_count, lambda k: row_return(h, g, k).wait_recv())
+            for source in range(res_count):
+                first = source * items + g * group
+                back = row_back[h, source, g].astype(F32).reshape(group, part_rows, channels)
+                after_row[first : first + group, rows] = (
+                    x_ref[source, g, :, rows] + back + row_shift[...]
+                )
+        for g in range(h * part_columns, (h + 1) * part_columns):
+            for part in range(seq_count):
+                here = after_row[:, g * seq_count + part, :]
+                after_turned[g, part] = here
+                col_sent[g, part] = standardize(here, gains[1:2], shifts[1:2])
+            each(seq_count, lambda k: col_copy(g, k).start())
+            col_in[g, me_seq] = col_sent[g, me_seq]
+
+    def attend_column(g):
         each(seq_count, lambda k: col_copy(g, k).wait_recv())
         result = attend(
             col_in[g].reshape(seq_count * seq_local, channels),
@@ -288,25 +309,35 @@
         )
         col_out[g] = result.astype(BF16).reshape(seq_count, seq_local, channels)
         each(seq_count, lambda k: col_return(g, k).start())
-        col_back[me_seq * columns + g] = col_out[g, me_seq]
+        col_back[g, me_seq] = col_out[g, me_seq]
+
+    send_columns(0)
+    attend_column(0)
+    for h in range(1, halves):
+        send_columns(h)
+    for g in range(1, columns):
+        attend_column(g)
 
     for i in (6, 7, 12, 13):
         loads[i].wait()
     for g in range(columns):
         each(seq_count, lambda k: col_return(g, k).wait_recv())
-        places = [part * columns + g for part in range(seq_count)]
-        done = jnp.concatenate(
-            [after_turned[j] + col_back[j].astype(F32) for j in places], axis=0
-        ) + col_shift[...]
+        tokens = seq_count * seq_local
+        done = (
+            after_turned[g].reshape(tokens, channels)
+            + col_back[g].astype(F32).reshape(tokens, channels)
+            + col_shift[...]
+        )
         normed = standardize(done, gains[2:3], shifts[2:3])
         inner = jnp.maximum(dot(normed, ff_first[...]) + ff_first_shift[...], 0.0).astype(BF16)
         final = done + dot(inner, ff_second[...]) + ff_second_shift[...]
-        for part, j in enumerate(places):
-            out_ref[:, j, :] = final[part * seq_local : (part + 1) * seq_local]
+        for part in range(seq_count):
+            out_ref[:, g * seq_count + part, :] = final[part * seq_local : (part + 1) * seq_local]
 
     for g in range(groups):
         each(res_count, lambda k: row_copy(g, k).wait_send())
-        each(res_count, lambda k: row_return(g, k).wait_send())
+        for h in range(halves):
+            each(res_count, lambda k: row_return(h, g, k).wait_send())
     for g in range(columns):
         each(seq_count, lambda k: col_copy(g, k).wait_send())
         each(seq_count, lambda k: col_return(g, k).wait_send())
@@ -337,6 +368,8 @@
     group = 2 if items % 2 == 0 else 1
     groups = items // group
     columns = res_local // seq_count
+    halves = 2 if columns % 2 == 0 and group % 2 == 0 and res_local % 16 == 0 else 1
+    part_rows = res_local // halves
     vmem = pl.BlockSpec(memory_space=pltpu.VMEM)
     in_hbm = pl.BlockSpec(memory_space=pltpu.HBM)
     row_length, col_length = res_local * res_count, seq_local * seq_count
@@ -374,19 +407,20 @@
             pltpu.VMEM((2, channels, channels), BF16),
             pltpu.VMEM((groups, res_count, group, res_local, channels), BF16),
             pltpu.VMEM((groups, res_count, group, res_local, channels), BF16),
-            pltpu.VMEM((groups, res_count, group, res_local, channels), BF16),
-            pltpu.VMEM((res_count, groups, group, res_local, channels), BF16),
+            pltpu.VMEM((halves, groups, res_count, group * part_rows, channels), BF16),
+            pltpu.VMEM((halves, res_count, groups, group * part_rows, channels), BF16),
             pltpu.VMEM((seq_local, res_local, channels), F32),
-            pltpu.VMEM((res_local, seq_local, channels), F32),
-            pltpu.VMEM((res_local, seq_local, channels), BF16),
+            pltpu.VMEM((columns, seq_count, seq_local, channels), F32),
             pltpu.VMEM((columns, seq_count, seq_local, channels), BF16),
             pltpu.VMEM((columns, seq_count, seq_local, channels), BF16),
-            pltpu.VMEM((res_local, seq_local, channels), BF16),
+            pltpu.VMEM((columns, seq_count, seq_local, channels), BF16),
+            pltpu.VMEM((columns, seq_count, seq_local, channels), BF16),
             mixed(row_length),
             mixed(col_length),
             pltpu.SemaphoreType.DMA((groups,)),
             pltpu.SemaphoreType.DMA((14,)),
-            pltpu.SemaphoreType.DMA((2, 2, groups, res_count)),
+            pltpu.SemaphoreType.DMA((1, 2, groups, res_count)),
+            pltpu.SemaphoreType.DMA((1, 2, halves * groups, res_count)),
             pltpu.SemaphoreType.DMA((2, 2, columns, seq_count)),
         ],
         compiler_params=pltpu.CompilerParams(

time: 41.4 us -> 43.4 us (1.048)
  Pallas kernels: 39.2 us -> 41.2 us
    pallas_call x1, Pallas kernels: 39.2 us -> 41.2 us  [shards(): pl.pallas_call(functools.partial(block, res_count, seq_count), out_shape=...]
where the time goes in v3:
time: 43.4 us; the launch traced here: 43.3 us
  Pallas kernels  41.2 us (95%)
  local copies, waits for them, and re-layouts  2.06 us (5%)
    pallas_call x1, Pallas kernels, shards(): pl.pallas_call(functools.partial(block, res_count, seq_count), out_shape=...  41.2 us
    unnamed x1, local copies, waits for them, and re-layouts  2.06 us

profile of v3, /device:TPU:0, one launch (start us, length us, event | category | flops | bytes accessed | tf_op | source)
XLA Modules:
  0.0 43.3 jit_solution(321265524600163881)
XLA Ops:
  0.0 41.2 %shard_map.145 = f32[48,16,256]{2,1,0:T(8,128)} custom-call(f32[8,3,2,16,256]{4,3,2,1,0:T(8,128)} %bitcast.7, f32[3,256]{1,0:T(4,128)} %gains_hbm.1, f32[3,256]{1,0:T(4,128)} %shifts_hbm.1, f32[1,256]{1,0:T(1,128)} %bitcast.9, f32[1,256]{1,0:T(1,128)} %bitcast.10, f32[1,256]{1,0:T(1,128)} %bitcast.11, f32[1,256]{1,0:T(1,128)} %bitcast.12, ...), custom_call_target="tpu_custom_call" | custom-call | flops 1811939328 | bytes 3145728 | tf_op jit(solution)/shard_map/pallas_call | solution.py:386
  41.2 2.1 %copy.17 = f32[48,16,256]{2,1,0:T(8,128)} copy(f32[48,16,256]{2,1,0:T(8,128)} %shard_map.145) | data formatting | bytes 1572864

commit v4 on v3

--- a/solution.py
+++ b/solution.py
@@ -135,7 +135,8 @@
     mixed_col,
     x_sem,
     load_sem,
-    sems,
+    send_sems,
+    row_sems,
     back_sems,
     col_sems,
 ):
@@ -152,13 +153,24 @@
 
     barrier = pltpu.get_barrier_semaphore()
 
+    def each(count, act):
+        if count <= 8:
+            for k in range(1, count):
+                act(k)
+        else:
+
+            def step(k, carry):
+                act(k)
+                return carry
+
+            lax.fori_loop(1, count, step, 0)
+
     def greet(axis, me, count):
-        def step(k, carry):
+        def act(k):
             peer = lax.rem(me + k, count)
             pl.semaphore_signal(barrier, inc=1, device_id={axis: peer}, device_id_type=MESH)
-            return carry
-
-        lax.fori_loop(1, count, step, 0)
+
+        each(count, act)
 
     greet("res", me_res, res_count)
     greet("seq", me_seq, seq_count)
@@ -188,51 +200,52 @@
     for load in loads[:2] + x_loads + loads[2:]:
         load.start()
 
-    def send(g, k, src, dst, axis, peer, sem, phase):
+    def send(src, dst, axis, peer, phase, recv_sem):
         return pltpu.make_async_remote_copy(
             src_ref=src,
             dst_ref=dst,
-            send_sem=sem.at[phase, 0, g, k],
-            recv_sem=sem.at[phase, 1, g, k],
+            send_sem=send_sems.at[phase],
+            recv_sem=recv_sem,
             device_id={axis: peer},
             device_id_type=MESH,
         )
 
     def row_copy(g, k):
         peer = lax.rem(me_res + k, res_count)
-        return send(g, k, row_sent.at[g, peer], row_in.at[g, me_res], "res", peer, sems, 0)
+        return send(
+            row_sent.at[g, peer], row_in.at[g, me_res], "res", peer, 0, row_sems.at[g]
+        )
 
     def row_return(h, g, k):
         peer = lax.rem(me_res + k, res_count)
         return send(
-            h * groups + g,
-            k,
             row_out.at[h, g, peer],
-            row_back.at[h, me_res, g],
+            row_back.at[h, g, me_res],
             "res",
             peer,
-            back_sems,
-            0,
+            1,
+            back_sems.at[h * groups + g],
         )
 
     def col_copy(g, k):
         peer = lax.rem(me_seq + k, seq_count)
         return send(
-            g, k, col_sent.at[g, peer], col_in.at[g, me_seq], "seq", peer, col_sems, 0
+            col_sent.at[g, peer], col_in.at[g, me_seq], "seq", peer, 2, col_sems.at[0, g]
         )
 
     def col_return(g, k):
         peer = lax.rem(me_seq + k, seq_count)
         return send(
-            g, k, col_out.at[g, peer], col_back.at[g, me_seq], "seq", peer, col_sems, 1
-        )
-
-    def each(count, act):
-        def step(k, carry):
-            act(k)
-            return carry
-
-        lax.fori_loop(1, count, step, 0)
+            col_out.at[g, peer], col_back.at[g, me_seq], "seq", peer, 3, col_sems.at[1, g]
+        )
+
+    def arrived(buffer, sem):
+        rest = buffer.at[pl.ds(0, buffer.shape[0] - 1)]
+        pltpu.make_async_copy(rest, rest, sem).wait()
+
+    def left(buffer, phase):
+        rest = buffer.at[:, pl.ds(0, buffer.shape[1] - 1)]
+        pltpu.make_async_copy(rest, rest, send_sems.at[phase]).wait()
 
     loads[0].wait()
     loads[1].wait()
@@ -248,7 +261,7 @@
         loads[i].wait()
     turned_value[0] = row_entry[:, 2 * channels : 3 * channels].T
     for g in range(groups):
-        each(res_count, lambda k: row_copy(g, k).wait_recv())
+        arrived(row_in.at[g], row_sems.at[g])
         result = attend(
             jnp.concatenate(
                 [row_in[g, :, i].reshape(row_length, channels) for i in range(group)], axis=0
@@ -273,7 +286,7 @@
             if g == groups - 1:
                 each(res_count, lambda k: row_return(h, g, k).start())
         for h in range(halves):
-            row_back[h, me_res, g] = row_out[h, g, me_res]
+            row_back[h, g, me_res] = row_out[h, g, me_res]
 
     for i in (4, 5, 10, 11):
         loads[i].wait()
@@ -281,10 +294,10 @@
     def send_columns(h):
         rows = slice(h * part_rows, (h + 1) * part_rows)
         for g in range(groups):
-            each(res_count, lambda k: row_return(h, g, k).wait_recv())
+            arrived(row_back.at[h, g], back_sems.at[h * groups + g])
             for source in range(res_count):
                 first = source * items + g * group
-                back = row_back[h, source, g].astype(F32).reshape(group, part_rows, channels)
+                back = row_back[h, g, source].astype(F32).reshape(group, part_rows, channels)
                 after_row[first : first + group, rows] = (
                     x_ref[source, g, :, rows] + back + row_shift[...]
                 )
@@ -297,7 +310,7 @@
             col_in[g, me_seq] = col_sent[g, me_seq]
 
     def attend_column(g):
-        each(seq_count, lambda k: col_copy(g, k).wait_recv())
+        arrived(col_in.at[g], col_sems.at[0, g])
         result = attend(
             col_in[g].reshape(seq_count * seq_local, channels),
             seq_count * seq_local,
@@ -321,7 +334,7 @@
     for i in (6, 7, 12, 13):
         loads[i].wait()
     for g in range(columns):
-        each(seq_count, lambda k: col_return(g, k).wait_recv())
+        arrived(col_back.at[g], col_sems.at[1, g])
         tokens = seq_count * seq_local
         done = (
             after_turned[g].reshape(tokens, channels)
@@ -334,13 +347,11 @@
         for part in range(seq_count):
             out_ref[:, g * seq_count + part, :] = final[part * seq_local : (part + 1) * seq_local]
 
-    for g in range(groups):
-        each(res_count, lambda k: row_copy(g, k).wait_send())
-        for h in range(halves):
-            each(res_count, lambda k: row_return(h, g, k).wait_send())
-    for g in range(columns):
-        each(seq_count, lambda k: col_copy(g, k).wait_send())
-        each(seq_count, lambda k: col_return(g, k).wait_send())
+    left(row_sent, 0)
+    for h in range(halves):
+        left(row_out.at[h], 1)
+    left(col_sent, 2)
+    left(col_out, 3)
 
 
 def shards(
@@ -368,7 +379,7 @@
     group = 2 if items % 2 == 0 else 1
     groups = items // group
     columns = res_local // seq_count
-    halves = 2 if columns % 2 == 0 and group % 2 == 0 and res_local % 16 == 0 else 1
+    halves = 1
     part_rows = res_local // halves
     vmem = pl.BlockSpec(memory_space=pltpu.VMEM)
     in_hbm = pl.BlockSpec(memory_space=pltpu.HBM)
@@ -408,7 +419,7 @@
             pltpu.VMEM((groups, res_count, group, res_local, channels), BF16),
             pltpu.VMEM((groups, res_count, group, res_local, channels), BF16),
             pltpu.VMEM((halves, groups, res_count, group * part_rows, channels), BF16),
-            pltpu.VMEM((halves, res_count, groups, group * part_rows, channels), BF16),
+            pltpu.VMEM((halves, groups, res_count, group * part_rows, channels), BF16),
             pltpu.VMEM((seq_local, res_local, channels), F32),
             pltpu.VMEM((columns, seq_count, seq_local, channels), F32),
             pltpu.VMEM((columns, seq_count, seq_local, channels), BF16),
@@ -419,9 +430,10 @@
             mixed(col_length),
             pltpu.SemaphoreType.DMA((groups,)),
             pltpu.SemaphoreType.DMA((14,)),
-            pltpu.SemaphoreType.DMA((1, 2, groups, res_count)),
-            pltpu.SemaphoreType.DMA((1, 2, halves * groups, res_count)),
-            pltpu.SemaphoreType.DMA((2, 2, columns, seq_count)),
+            pltpu.SemaphoreType.DMA((4,)),
+            pltpu.SemaphoreType.DMA((groups,)),
+            pltpu.SemaphoreType.DMA((halves * groups,)),
+            pltpu.SemaphoreType.DMA((2, columns)),
         ],
         compiler_params=pltpu.CompilerParams(
             collective_id=0, has_side_effects=True, vmem_limit_bytes=63 * 1024 * 1024

time: 43.4 us -> 39.6 us (0.912)
  Pallas kernels: 41.2 us -> 37.4 us
    pallas_call x1, Pallas kernels: 41.2 us -> 37.4 us  [shards(): pl.pallas_call(functools.partial(block, res_count, seq_count), out_shape=...]
where the time goes in v4:
time: 39.6 us; the launch traced here: 39.4 us
  Pallas kernels  37.4 us (94%)
  local copies, waits for them, and re-layouts  2.06 us (5%)
    pallas_call x1, Pallas kernels, shards(): pl.pallas_call(functools.partial(block, res_count, seq_count), out_shape=...  37.4 us
    unnamed x1, local copies, waits for them, and re-layouts  2.06 us

profile of v4, /device:TPU:0, one launch (start us, length us, event | category | flops | bytes accessed | tf_op | source)
XLA Modules:
  0.0 39.4 jit_solution(588899161742493426)
XLA Ops:
  0.0 37.4 %shard_map.145 = f32[48,16,256]{2,1,0:T(8,128)} custom-call(f32[8,3,2,16,256]{4,3,2,1,0:T(8,128)} %bitcast.7, f32[3,256]{1,0:T(4,128)} %gains_hbm.1, f32[3,256]{1,0:T(4,128)} %shifts_hbm.1, f32[1,256]{1,0:T(1,128)} %bitcast.9, f32[1,256]{1,0:T(1,128)} %bitcast.10, f32[1,256]{1,0:T(1,128)} %bitcast.11, f32[1,256]{1,0:T(1,128)} %bitcast.12, ...), custom_call_target="tpu_custom_call" | custom-call | flops 1811939328 | bytes 3145728 | tf_op jit(solution)/shard_map/pallas_call | solution.py:397
  37.4 2.1 %copy.17 = f32[48,16,256]{2,1,0:T(8,128)} copy(f32[48,16,256]{2,1,0:T(8,128)} %shard_map.145) | data formatting | bytes 1572864

commit v5 on v4

--- a/solution.py
+++ b/solution.py
@@ -345,7 +345,9 @@
         inner = jnp.maximum(dot(normed, ff_first[...]) + ff_first_shift[...], 0.0).astype(BF16)
         final = done + dot(inner, ff_second[...]) + ff_second_shift[...]
         for part in range(seq_count):
-            out_ref[:, g * seq_count + part, :] = final[part * seq_local : (part + 1) * seq_local]
+            after_row[:, g * seq_count + part, :] = final[part * seq_local : (part + 1) * seq_local]
+
+    out_ref[...] = after_row[...].astype(BF16)
 
     left(row_sent, 0)
     for h in range(halves):
@@ -396,7 +398,7 @@
     tokens = seq_local * res_local
     return pl.pallas_call(
         functools.partial(block, res_count, seq_count),
-        out_shape=jax.ShapeDtypeStruct(alignment_tensor.shape, F32),
+        out_shape=jax.ShapeDtypeStruct(alignment_tensor.shape, BF16),
         in_specs=[in_hbm] * 15,
         out_specs=vmem,
         scratch_shapes=[
@@ -459,7 +461,7 @@
         vertical_exit_matrix,
         feedforward_first_matrix,
         feedforward_second_matrix,
-    )
+    ).astype(F32)
 
 
 def solution(mesh):

time: 39.6 us -> 39.4 us (level)
  local copies, waits for them, and re-layouts: 2.06 us -> 0 us
  other arithmetic: 0 us -> 1.98 us
    unnamed x1 -> x0, local copies, waits for them, and re-layouts: 2.06 us -> none
    convert_element_type x0 -> x1, other arithmetic: none -> 1.98 us  [shards(): return pl.pallas_call(functools.partial(block, res_count, seq_count), out...]
where the time goes in v5:
time: 39.4 us; the launch traced here: 39.3 us
  Pallas kernels  37.3 us (95%)
  other arithmetic  1.98 us (5%)
    pallas_call x1, Pallas kernels, shards(): pl.pallas_call(functools.partial(block, res_count, seq_count), out_shape=...  37.3 us
    convert_element_type x1, other arithmetic, shards(): return pl.pallas_call(functools.partial(block, res_count, seq_count), out...  1.98 us

profile of v5, /device:TPU:0, one launch (start us, length us, event | category | flops | bytes accessed | tf_op | source)
XLA Modules:
  0.0 39.3 jit_solution(17866118373541040066)
XLA Ops:
  0.0 37.3 %shard_map.145 = bf16[48,16,256]{2,1,0:T(8,128)(2,1)} custom-call(f32[8,3,2,16,256]{4,3,2,1,0:T(8,128)} %bitcast.7, f32[3,256]{1,0:T(4,128)} %gains_hbm.1, f32[3,256]{1,0:T(4,128)} %shifts_hbm.1, f32[1,256]{1,0:T(1,128)} %bitcast.9, f32[1,256]{1,0:T(1,128)} %bitcast.10, f32[1,256]{1,0:T(1,128)} %bitcast.11, f32[1,256]{1,0:T(1,128)} %bitcast.12, ...), custom_call_target="tpu_custom_call" | custom-call | flops 1811939328 | bytes 3145728 | tf_op jit(solution)/shard_map/pallas_call | solution.py:399
  37.3 2.0 %convert_element_type.3 = f32[48,16,256]{2,1,0:T(8,128)} convert(bf16[48,16,256]{2,1,0:T(8,128)(2,1)} %shard_map.145) | non-fusion elementwise | flops 196608 | bytes 1179648 | tf_op jit(solution)/shard_map/convert_element_type | solution.py:464
